TPU v7x, 32 devices: a whole 2x2x4 slice. The times are simulated.
32 devices in a mesh: dp: 4 (over x, core), sx: 2 (over y), sy: 4 (over z).
Axes of the slice: x: 2, y: 2, z: 4, core: 2. Of those that a mesh axis runs over, the one named last changes fastest.
Arguments:
- volume: bfloat16 [4, 32, 64, 32, 128], P('dp', 'sx', 'sy'), may hold values from -6 to 6
- block_active: int32 [4, 2, 4, 2], P('dp', 'sx', 'sy'), may hold values from 0 to 1, as said below
- weight: bfloat16 [3, 3, 3, 128, 128], replicated, may hold values from -0.109375 to 0.109375
- bias: float32 [128], replicated, may hold values from -3 to 3
- cotangent: bfloat16 [4, 32, 64, 32, 128], P('dp', 'sx', 'sy'), may hold values from -0.01171875 to 0.01171875
Outputs:
- activated: bfloat16 [4, 32, 64, 32, 128], P('dp', 'sx', 'sy')
- grad_weight: float32 [3, 3, 3, 128, 128], replicated
- grad_bias: float32 [128], replicated
Inputs may be any that keep to these rules, and one draw needn't show every extreme that they name: `block_active`: every tile of 2 blocks along depth (one value of the first three indices) has at least one active block; the number of active blocks of a tile is drawn evenly from 1 to 2.
All inputs are finite; a program needn't handle non-finite values.
Results may differ from a plain program's by a relative error of at most 0.006.
Values may be sent and summed in bfloat16 or wider, within the bound.
A program may use at most 64 MiB of HBM per device.

v0:
```python
import jax
import jax.numpy as jnp
from jax import lax
from jax.sharding import PartitionSpec as P


def with_halo(block, sides, width):
    for axis, dim in sides:
        count = lax.axis_size(axis)
        forward = [(i, i + 1) for i in range(count - 1)]
        backward = [(target, source) for source, target in forward]
        low = lax.ppermute(
            lax.slice_in_dim(block, block.shape[dim] - width, None, axis=dim), axis, forward
        )
        high = lax.ppermute(lax.slice_in_dim(block, 0, width, axis=dim), axis, backward)
        block = jnp.concatenate([low, block, high], axis=dim)
    return block


def layer_work(slab, cot_piece, vox_mask, weight, bias):
    pre = (
        lax.conv_general_dilated(
            slab,
            weight,
            (1, 1, 1),
            "VALID",
            dimension_numbers=("NDHWC", "DHWIO", "NDHWC"),
            preferred_element_type=jnp.float32,
        )
        + bias
    )
    sig = jax.nn.sigmoid(pre)
    out = (pre * sig * vox_mask).astype(jnp.bfloat16)
    dpre = (cot_piece.astype(jnp.float32) * sig * (1.0 + pre * (1.0 - sig)) * vox_mask).astype(
        jnp.bfloat16
    )
    span_x = cot_piece.shape[1]
    span_y = cot_piece.shape[2]
    span_z = cot_piece.shape[3]
    channels = cot_piece.shape[4]
    grads = []
    for a in range(3):
        for b in range(3):
            for c in range(3):
                piece = slab[:, a : a + span_x, b : b + span_y, c : c + span_z, :]
                grads.append(
                    lax.dot_general(
                        piece,
                        dpre,
                        (((0, 1, 2, 3), (0, 1, 2, 3)), ((), ())),
                        preferred_element_type=jnp.float32,
                    )
                )
    grad_w = jnp.stack(grads).reshape(3, 3, 3, channels, channels)
    grad_b = jnp.sum(dpre.astype(jnp.float32), axis=(0, 1, 2, 3))
    return (out, grad_w, grad_b)


def local(volume, block_active, weight, bias, cotangent):
    depth = volume.shape[3]
    blocks = block_active.shape[3]
    edge = depth // blocks
    vox_mask = jnp.repeat(block_active, edge, axis=3)[..., None].astype(jnp.float32)
    masked = volume * vox_mask.astype(jnp.bfloat16)
    padded = with_halo(masked, (("sx", 1), ("sy", 2)), 1)
    padded = jnp.pad(padded, ((0, 0), (0, 0), (0, 0), (1, 1), (0, 0)))
    activated, grad_w, grad_b = layer_work(padded, cotangent, vox_mask, weight, bias)
    grad_w, grad_b = lax.psum((grad_w, grad_b), ("dp", "sx", "sy"))
    return (activated, grad_w, grad_b)


def solution(mesh):
    placed = (
        P("dp", "sx", "sy", None, None),
        P("dp", "sx", "sy", None),
        P(),
        P(),
        P("dp", "sx", "sy", None, None),
    )
    return jax.shard_map(
        local,
        mesh=mesh,
        in_specs=placed,
        out_specs=(P("dp", "sx", "sy", None, None), P(), P()),
        check_vma=False,
    )
```

profile of v0, /device:TPU:0, one launch (start us, length us, event | category | flops | bytes accessed | tf_op | source)
XLA Modules:
  0.0 235.1 jit_solution(5884322632707149575)
XLA Ops:
  8.1 1.8 broadcast_multiply_fusion
  9.9 4.9 %collective-permute-start = (bf16[1,1,16,32,128]{4,3,2,1,0:T(8,128)(2,1)S(1)}, bf16[1,1,16,32,128]{4,3,2,1,0:T(8,128)(2,1)S(1)}, u32[]{:S(2)}, u32[]{:S(2)}) collective-permute-start(bf16[1,1,16,32,128]{4,3,2,1,0:T(8,128)(2,1)S(1)} %get-tuple-element.15), channel_id=1, source_target_pairs={{0,4},{1,5},{2,6},{3,7},{8,12},{9,13},{10,14},{11,15},{16,20},{17,... | collective-permute-start | bytes 393224 | tf_op jit(solution)/shard_map/ppermute | solution.py:12
  14.8 1.3 collective-permute-start.1
  16.1 1.4 collective-permute-done
  17.6 4.1 %collective-permute-done.1 = bf16[1,1,16,32,128]{4,3,2,1,0:T(8,128)(2,1)S(1)} collective-permute-done((bf16[1,1,16,32,128]{4,3,2,1,0:T(8,128)(2,1)S(1)}, bf16[1,1,16,32,128]{4,3,2,1,0:T(8,128)(2,1)S(1)}, u32[]{:S(2)}, u32[]{:S(2)}) %collective-permute-start.1) | collective-permute-done | bytes 131104 | tf_op jit(solution)/shard_map/ppermute | solution.py:15
  21.7 3.5 %collective-permute-start.2 = (bf16[1,18,1,32,128]{4,3,2,1,0:T(8,128)(2,1)S(1)}, bf16[1,18,1,32,128]{4,3,2,1,0:T(8,128)(2,1)S(1)}, u32[]{:S(2)}, u32[]{:S(2)}) collective-permute-start(bf16[1,18,1,32,128]{4,3,2,1,0:T(8,128)(2,1)S(1)} %get-tuple-element.13), channel_id=1, source_target_pairs={{0,1},{1,2},{2,3},{4,5},{5,6},{6,7},{8,9},{9,10},{10,11},{12,13},{... | collective-permute-start | bytes 442376 | tf_op jit(solution)/shard_map/ppermute | solution.py:12
  25.2 1.3 collective-permute-start.3
  26.5 1.3 collective-permute-done.2
  27.9 4.4 %collective-permute-done.3 = bf16[1,18,1,32,128]{4,3,2,1,0:T(8,128)(2,1)S(1)} collective-permute-done((bf16[1,18,1,32,128]{4,3,2,1,0:T(8,128)(2,1)S(1)}, bf16[1,18,1,32,128]{4,3,2,1,0:T(8,128)(2,1)S(1)}, u32[]{:S(2)}, u32[]{:S(2)}) %collective-permute-start.3) | collective-permute-done | bytes 147488 | tf_op jit(solution)/shard_map/ppermute | solution.py:15
  32.8 1.3 copy.70
  36.2 22.2 %add_divide_fusion = (f32[16,16,8,5,128]{4,2,3,1,0:T(8,128)S(1)}, f32[16,16,8,5,128]{4,2,3,1,0:T(8,128)}, f32[16,16,8,5,128]{4,2,3,1,0:T(8,128)S(1)}) fusion(f32[128]{0:T(128)S(1)} %copy-done.4, pred[8,5]{0,1:T(8,128)(4,1)S(1)} %copy-done.5, bf16[3,3,3,128,128]{4,3,2,1,0:T(8,128)(2,1)S(1)} %copy-done, bf16[18,18,1,7,2,128]{5,3,4,1,0,2:T(8,128)(2,1)S(1)} %slice.147, ...), kind=kOutput, calls=%fused_computation.3 | convolution fusion | flops 9085427712 | bytes 21092904 | tf_op jit(solution)/shard_map/conv_general_dilated | solution.py:22
  60.9 1.9 convert_reduce_fusion
  66.2 1.1 fusion.215
  69.2 1.1 fusion.203
  70.4 1.1 fusion.197
  72.3 1.1 fusion.191
  73.4 1.1 fusion.185
  75.3 1.1 fusion.179
  78.5 1.1 fusion.167
  79.6 1.1 fusion.161
  81.5 1.1 fusion.155
  82.6 1.1 fusion.149
  84.5 1.1 fusion.143
  87.5 1.1 fusion.131
  88.7 1.1 fusion.125
  90.8 1.1 fusion.119
  91.9 1.2 copy-done.3
  93.2 3.4 %copy.11 = f32[16,16,8,5,128]{4,1,3,2,0:T(8,128)S(1)} copy(f32[16,16,8,5,128]{4,2,3,1,0:T(8,128)} %get-tuple-element.9) | data formatting | bytes 10485760 | tf_op jit(solution)/shard_map/mul | solution.py:33
  97.1 1.9 copy.42
  99.0 39.7 %psum.15 = f32[128]{0:T(128)} all-reduce(f32[128]{0:T(128)S(1)} %get-tuple-element.6), channel_id=1, replica_groups=mesh['dp'=4,'sx'=2,'sy'=4] {'dp','sx','sy'}, use_global_device_ids=true, to_apply=%region_2.3 | all-reduce | flops 128 | bytes 1024 | tf_op jit(solution)/shard_map/psum | solution.py:68
  138.7 86.5 %all-reduce.3.cloned.1.call-done = f32[3,3,3,128,128]{4,3,2,1,0:T(8,128)} async-done(((f32[3,3,3,128,128]{4,3,2,1,0:T(8,128)}), f32[3,3,3,128,128]{4,3,2,1,0:T(8,128)}) %all-reduce.3.cloned.1.call-update) | async-done | bytes 1769488 | tf_op jit(solution)/shard_map/psum | solution.py:68
  225.1 2.9 %copy.154 = f32[3,3,3,128,128]{4,3,2,1,0:T(8,128)} copy(f32[3,3,3,128,128]{4,3,2,1,0:T(8,128)} %all-reduce.3.cloned.1.call-done) | data formatting | bytes 3538944
  (41 shorter events, 19.8 us)
Async XLA Ops:
  7.2 28.7 %copy-start = (bf16[3,3,3,128,128]{4,3,2,1,0:T(8,128)(2,1)S(1)}, bf16[3,3,3,128,128]{4,3,2,1,0:T(8,128)(2,1)}, u32[]{:S(2)}) copy-start(bf16[3,3,3,128,128]{4,3,2,1,0:T(8,128)(2,1)} %param.7) | copy-start | bytes 2654212
  7.2 217.9 %all-reduce.3.cloned.1.call-start = ((), (), s32[]{:S(2)}) async-start(), calls=%async_computation | async-start | bytes 3538944 | tf_op jit(solution)/shard_map/psum | solution.py:68
  9.9 7.6 %collective-permute-start = (bf16[1,1,16,32,128]{4,3,2,1,0:T(8,128)(2,1)S(1)}, bf16[1,1,16,32,128]{4,3,2,1,0:T(8,128)(2,1)S(1)}, u32[]{:S(2)}, u32[]{:S(2)}) collective-permute-start(bf16[1,1,16,32,128]{4,3,2,1,0:T(8,128)(2,1)S(1)} %get-tuple-element.15), channel_id=1, source_target_pairs={{0,4},{1,5},{2,6},{3,7},{8,12},{9,13},{10,14},{11,15},{16,20},{17,... | collective-permute-start | bytes 393224 | tf_op jit(solution)/shard_map/ppermute | solution.py:12
  14.8 6.9 %collective-permute-start.1 = (bf16[1,1,16,32,128]{4,3,2,1,0:T(8,128)(2,1)S(1)}, bf16[1,1,16,32,128]{4,3,2,1,0:T(8,128)(2,1)S(1)}, u32[]{:S(2)}, u32[]{:S(2)}) collective-permute-start(bf16[1,1,16,32,128]{4,3,2,1,0:T(8,128)(2,1)S(1)} %get-tuple-element.16), channel_id=1, source_target_pairs={{4,0},{5,1},{6,2},{7,3},{12,8},{13,9},{14,10},{15,11},{20,16},{21,... | collective-permute-start | bytes 393224 | tf_op jit(solution)/shard_map/ppermute | solution.py:15
  21.7 6.1 %collective-permute-start.2 = (bf16[1,18,1,32,128]{4,3,2,1,0:T(8,128)(2,1)S(1)}, bf16[1,18,1,32,128]{4,3,2,1,0:T(8,128)(2,1)S(1)}, u32[]{:S(2)}, u32[]{:S(2)}) collective-permute-start(bf16[1,18,1,32,128]{4,3,2,1,0:T(8,128)(2,1)S(1)} %get-tuple-element.13), channel_id=1, source_target_pairs={{0,1},{1,2},{2,3},{4,5},{5,6},{6,7},{8,9},{9,10},{10,11},{12,13},{... | collective-permute-start | bytes 442376 | tf_op jit(solution)/shard_map/ppermute | solution.py:12
  25.2 7.0 %collective-permute-start.3 = (bf16[1,18,1,32,128]{4,3,2,1,0:T(8,128)(2,1)S(1)}, bf16[1,18,1,32,128]{4,3,2,1,0:T(8,128)(2,1)S(1)}, u32[]{:S(2)}, u32[]{:S(2)}) collective-permute-start(bf16[1,18,1,32,128]{4,3,2,1,0:T(8,128)(2,1)S(1)} %get-tuple-element.14), channel_id=1, source_target_pairs={{1,0},{2,1},{3,2},{5,4},{6,5},{7,6},{9,8},{10,9},{11,10},{13,12},{... | collective-permute-start | bytes 442376 | tf_op jit(solution)/shard_map/ppermute | solution.py:15
  35.5 0.7 copy-start.4
  35.5 0.7 copy-start.5
  59.3 1.6 copy-start.2
  91.9 1.2 copy-start.3
  97.1 130.9 %copy-start.1 = (bf16[3,3,3,128,128]{4,3,2,1,0:T(8,128)(2,1)S(1)}, bf16[3,3,3,128,128]{4,3,2,1,0:T(8,128)(2,1)}, u32[]{:S(2)}) copy-start(bf16[3,3,3,128,128]{4,3,2,1,0:T(8,128)(2,1)} %param.7) | copy-start | bytes 2654212
Sparse Core Ops, SparseCore 0:
  93.3 131.7 all-reduce.2
where the time goes:
time: 239 us; the launch traced here: 235 us
  waiting for transfers between devices  97.8 us (41%)
  matrix products  49.7 us (21%)
  blocking collectives  39.7 us (17%)
  local copies, waits for them, and re-layouts  15.3 us (6%)
  between operations  14.6 us (6%)
  starting transfers between devices  11 us (5%)
  other arithmetic  7.05 us (3%)
    psum x1, waiting for transfers between devices, local(): grad_w, grad_b = lax.psum((grad_w, grad_b), ('dp', 'sx', 'sy'))  86.5 us
    psum x1, blocking collectives, local(): grad_w, grad_b = lax.psum((grad_w, grad_b), ('dp', 'sx', 'sy'))  39.7 us
    dot_general x27, matrix products, layer_work(): lax.dot_general(piece, dpre, (((0, 1, 2, 3), (0, 1, 2, 3)), ((), ())), pr...  27.4 us
    conv_general_dilated x1, matrix products, layer_work(): lax.conv_general_dilated(slab, weight, (1, 1, 1), 'VALID', dimension_numb...  22.2 us
    ppermute x2, waiting for transfers between devices, with_halo(): lax.ppermute(lax.slice_in_dim(block, 0, width, axis=dim), axis, backward)  8.52 us
    ppermute x2, starting transfers between devices, with_halo(): lax.ppermute(lax.slice_in_dim(block, block.shape[dim] - width, None, axis...  8.37 us
    unnamed x15, local copies, waits for them, and re-layouts  8.22 us
  transfers between devices with their start and end apart: 5, of which 5 were waited for; matrix products, arithmetic and copies ran while one was open for 2% of the time, Pallas kernels for 0%

commit v1 on v0

v1 whole, which is shorter than its diff:
```python
import functools

import jax
import jax.numpy as jnp
from jax import lax
from jax.experimental import pallas as pl
from jax.experimental.pallas import tpu as pltpu
from jax.sharding import PartitionSpec as P

MESH = pl.DeviceIdType.MESH
VM = pl.BlockSpec(memory_space=pltpu.VMEM)
SM = pl.BlockSpec(memory_space=pltpu.SMEM)
NEAR = [(dx, dy) for dx in (-1, 0, 1) for dy in (-1, 0, 1) if (dx, dy) != (0, 0)]
BF = jnp.bfloat16
F32 = jnp.float32


def depth_mask(act_ref, rows, depth, edge):
    z = lax.rem(lax.broadcasted_iota(jnp.int32, (rows, 128), 0), depth)
    m = jnp.zeros((rows, 128), F32)
    for k in range(depth // edge):
        inside = jnp.logical_and(z >= k * edge, z < (k + 1) * edge)
        m = jnp.where(inside, act_ref[k].astype(F32), m)
    return m


def halo_kernel(nsx, nsy, edge, act_ref, vol_ref, hx_ref, hy_ref, fx, fy, send, recv):
    nx, ny, nz, _ = vol_ref.shape
    ix, iy = lax.axis_index("sx"), lax.axis_index("sy")

    def there(dx, dy):
        x, y = ix + dx, iy + dy
        return (x >= 0) & (x < nsx) & (y >= 0) & (y < nsy)

    barrier = pltpu.get_barrier_semaphore()
    for dx, dy in NEAR:
        @pl.when(there(dx, dy))
        def _():
            pl.semaphore_signal(barrier, inc=1, device_id={"sx": ix + dx, "sy": iy + dy},
                                device_id_type=MESH)
    mask = depth_mask(act_ref, nz, nz, edge)[None].astype(BF)
    for side in range(2):
        fx[side] = vol_ref[side * (nx - 1)] * mask
        fy[side] = vol_ref[:, side * (ny - 1)] * mask
    pl.semaphore_wait(barrier, sum(there(dx, dy).astype(jnp.int32) for dx, dy in NEAR))

    def slot(dx, dy):
        if dy == 0:
            return hx_ref.at[int(dx > 0)]
        if dx == 0:
            return hy_ref.at[int(dy > 0), pl.ds(1, nx)]
        return hy_ref.at[int(dy > 0), (nx + 1) * int(dx > 0)]

    def copy(k):
        dx, dy = NEAR[k]
        if dy == 0:
            src = fx.at[int(dx > 0)]
        elif dx == 0:
            src = fy.at[int(dy > 0)]
        else:
            src = fx.at[int(dx > 0), (ny - 1) * int(dy > 0)]
        opp = NEAR.index((-dx, -dy))
        return pltpu.make_async_remote_copy(
            src_ref=src, dst_ref=slot(-dx, -dy), send_sem=send.at[k], recv_sem=recv.at[opp],
            device_id={"sx": ix + dx, "sy": iy + dy}, device_id_type=MESH)

    for k, (dx, dy) in enumerate(NEAR):
        @pl.when(there(dx, dy))
        def _():
            copy(k).start()

        @pl.when(jnp.logical_not(there(dx, dy)))
        def _():
            ref = slot(dx, dy)
            ref[...] = jnp.zeros(ref.shape, BF)
    for k, (dx, dy) in enumerate(NEAR):
        @pl.when(there(dx, dy))
        def _():
            copy(k).wait_send()
            copy(NEAR.index((-dx, -dy))).wait_recv()


def work_kernel(nz, edge, act_ref, vol_ref, hx_ref, hy_ref, w_ref, bias_ref, cot_ref,
                out_ref, g_ref, cols, dpt, acc):
    nx, rows, ch = vol_ref.shape
    full = rows + 2 * nz
    mask = depth_mask(act_ref, rows, nz, edge)
    maskb = mask.astype(BF)
    mid = slice(ch, 2 * ch)
    z = lax.rem(lax.broadcasted_iota(jnp.int32, (full, ch), 0), nz)
    first, last = z == 0, z == nz - 1

    cols[0, nz:nz + rows, mid] = hx_ref[0]
    cols[nx + 1, nz:nz + rows, mid] = hx_ref[1]

    @pl.loop(0, nx)
    def _(i):
        cols[i + 1, nz:nz + rows, mid] = vol_ref[i] * maskb

    @pl.loop(0, nx + 2)
    def _(i):
        cols[i, 0:nz, mid] = hy_ref[0, i]
        cols[i, nz + rows:full, mid] = hy_ref[1, i]
        v = cols[i, :, mid].astype(F32)
        cols[i, :, 0:ch] = jnp.where(first, 0.0, pltpu.roll(v, 1, 0)).astype(BF)
        cols[i, :, 2 * ch:3 * ch] = jnp.where(last, 0.0, pltpu.roll(v, full - 1, 0)).astype(BF)

    dpt[0:2 * ch, :] = jnp.zeros((2 * ch, rows), BF)
    dpt[(nx + 2) * ch:(nx + 4) * ch, :] = jnp.zeros((2 * ch, rows), BF)
    half = 6 * 3 * ch

    def pair(p, gb):
        pre = jnp.zeros((rows, 2 * ch), F32) + bias_ref[...]
        for j in range(2):
            lhs = jnp.concatenate(
                [cols[2 * p + 2 * j + t, pl.ds(b * nz, rows), :] for t in range(2) for b in range(3)], axis=1)
            pre = pre + jnp.dot(lhs, w_ref[j * half:(j + 1) * half, :], preferred_element_type=F32)
        for t in range(2):
            y = pre[:, t * ch:(t + 1) * ch]
            sig = jax.nn.sigmoid(y)
            out_ref[2 * p + t] = (y * sig * mask).astype(BF)
            d = (cot_ref[2 * p + t].astype(F32) * sig * (1.0 + y * (1.0 - sig)) * mask).astype(BF)
            gb = gb + jnp.sum(d.astype(F32), axis=0, keepdims=True)
            dpt[pl.ds(pl.multiple_of((2 * p + t + 2) * ch, ch), ch), :] = d.T
        return gb

    gb = lax.fori_loop(0, nx // 2, pair, jnp.zeros((1, ch), F32))
    acc[...] = jnp.zeros(acc.shape, F32)

    @pl.loop(0, nx + 2)
    def _(i):
        lhs = dpt[pl.ds(pl.multiple_of(i * ch, ch), 3 * ch), :]
        rhs = jnp.concatenate([cols[i, pl.ds(b * nz, rows), :] for b in range(3)], axis=1)
        acc[...] += jnp.dot(lhs, rhs, preferred_element_type=F32)

    for a in range(3):
        for q in range(9):
            g_ref[a * 9 + q] = acc[(2 - a) * ch:(3 - a) * ch, q * ch:(q + 1) * ch].T
    g_ref[27] = jnp.broadcast_to(gb, (ch, ch))


def reduce_kernel(nsx, chunks, g_ref, out_ref, s1, r1, a1, s2, r2, a2, s3, r3, s4, fin,
                  ss, rs):
    d, x, y = lax.axis_index("dp"), lax.axis_index("sx"), lax.axis_index("sy")
    h, dh = lax.rem(d, 2), d // 2
    xl, xh = lax.rem(x, 2), x // 2
    q = dh * 2 + xl
    far = nsx // 2

    def peer1():
        return {"dp": dh * 2 + 1 - h, "sx": x, "sy": y}

    def peer2(k):
        o = lax.rem(q + k, 4)
        return o, {"dp": (o // 2) * 2 + h, "sx": xh * 2 + lax.rem(o, 2), "sy": y}

    def peer3(k):
        o = lax.rem(y + k, 4)
        return o, {"dp": d, "sx": x, "sy": o}

    def peer4(k):
        o = lax.rem(xh + k, far)
        return o, {"dp": d, "sx": o * 2 + xl, "sy": y}

    peers = [peer1()] + [peer2(k)[1] for k in (1, 2, 3)] + [peer3(k)[1] for k in (1, 2, 3)]
    peers += [peer4(k)[1] for k in range(1, far)]
    barrier = pltpu.get_barrier_semaphore()
    for p in peers:
        pl.semaphore_signal(barrier, inc=1, device_id=p, device_id_type=MESH)

    def rcopy(src, dst, c, n, p):
        return pltpu.make_async_remote_copy(src_ref=src, dst_ref=dst, send_sem=ss.at[c, n],
                                            recv_sem=rs.at[c, n], device_id=p, device_id_type=MESH)

    def part(c):
        off, size = chunks[c]
        return pl.ds(off, size)

    def c1(c):
        return [rcopy(s1.at[:, part(c)], r1.at[:, part(c)], c, 0, peer1())]

    def c2(c):
        cs = []
        for k in (1, 2, 3):
            o, p = peer2(k)
            cs.append(rcopy(s2.at[o, :, part(c)], r2.at[k, :, part(c)], c, k, p))
        return cs

    def c3(c):
        cs = []
        for k in (1, 2, 3):
            o, p = peer3(k)
            cs.append(rcopy(s3.at[o, part(c)], r3.at[k, part(c)], c, 3 + k, p))
        return cs

    def c4(c):
        cs = []
        for k in range(1, far):
            o, p = peer4(k)
            cs.append(rcopy(s4.at[xh, part(c)], s4.at[xh, part(c)], c, 13 + k, p))
        return cs

    def c4in(c):
        cs = []
        for k in range(1, far):
            o, p = peer4(far - k)
            cs.append(rcopy(s4.at[xh, part(c)], s4.at[o, part(c)], c, 13 + k, p))
        return cs

    def g3(c, inn=False):
        cs = []
        for k in (1, 2, 3):
            o, p = peer3(4 - k if inn else k)
            cs.append(rcopy(fin.at[h, q, y, part(c)], fin.at[h, q, o if inn else y, part(c)], c, 6 + k, p))
        return cs

    def g2(c, inn=False):
        cs = []
        for k in (1, 2, 3):
            o, p = peer2(4 - k if inn else k)
            cs.append(rcopy(fin.at[h, q, :, part(c)], fin.at[h, o if inn else q, :, part(c)], c, 9 + k, p))
        return cs

    def g1(c, inn=False):
        return [rcopy(fin.at[h, :, :, part(c)], fin.at[1 - h if inn else h, :, :, part(c)], c, 13, peer1())]

    def start(cs):
        for r in cs:
            r.start()

    def landed(cs):
        for r in cs:
            r.wait_recv()

    def st0(c):
        s1[:, part(c)] = g_ref[1 - h, :, part(c)].astype(BF)
        if c == 0:
            pl.semaphore_wait(barrier, len(peers))
        start(c1(c))

    def st1(c):
        landed(c1(c))
        v = g_ref[h, :, part(c)] + r1[:, part(c)].astype(F32)
        v = v.reshape((4, 4) + v.shape[1:])
        a1[:, :, part(c)] = v
        s2[:, :, part(c)] = v.astype(BF)
        start(c2(c))

    def st2(c):
        landed(c2(c))
        v = a1[q, :, part(c)]
        for k in (1, 2, 3):
            v = v + r2[k, :, part(c)].astype(F32)
        a2[:, part(c)] = v
        s3[:, part(c)] = v.astype(BF)
        start(c3(c))

    def st3(c):
        landed(c3(c))
        v = a2[y, part(c)]
        for k in (1, 2, 3):
            v = v + r3[k, part(c)].astype(F32)
        if far > 1:
            s4[xh, part(c)] = v.astype(BF)
            start(c4(c))
            landed(c4in(c))
            v = s4[0, part(c)].astype(F32)
            for k in range(1, far):
                v = v + s4[k, part(c)].astype(F32)
        fin[h, q, y, part(c)] = v.astype(BF)
        start(g3(c))

    def st4(c):
        landed(g3(c, True))
        start(g2(c))

    def st5(c):
        landed(g2(c, True))
        start(g1(c))

    def st6(c):
        landed(g1(c, True))
        out_ref[:, :, :, part(c)] = fin[:, :, :, part(c)].astype(F32)

    stages = [st0, st1, st2, st3, st4, st5, st6]
    n = len(chunks)
    for t in range(n + len(stages) - 1):
        for s in reversed(range(len(stages))):
            if 0 <= t - s < n:
                stages[s](t - s)
    for c in range(n):
        for cs in (c1(c), c2(c), c3(c), c4(c), g3(c), g2(c), g1(c)):
            for r in cs:
                r.wait_send()


def local(nsx, nsy, volume, block_active, weight, bias, cotangent):
    _, nx, ny, nz, ch = volume.shape
    blocks = block_active.shape[3]
    edge = nz // blocks
    act = block_active.reshape(blocks)
    big = pltpu.CompilerParams(vmem_limit_bytes=60 * 2**20)
    hx, hy = pl.pallas_call(
        functools.partial(halo_kernel, nsx, nsy, edge),
        out_shape=(jax.ShapeDtypeStruct((2, ny, nz, ch), BF),
                   jax.ShapeDtypeStruct((2, nx + 2, nz, ch), BF)),
        in_specs=[SM, VM], out_specs=(VM, VM),
        scratch_shapes=[pltpu.VMEM((2, ny, nz, ch), BF), pltpu.VMEM((2, nx, nz, ch), BF),
                        pltpu.SemaphoreType.DMA((8,)), pltpu.SemaphoreType.DMA((8,))],
        compiler_params=pltpu.CompilerParams(collective_id=0, has_side_effects=True,
                                             vmem_limit_bytes=32 * 2**20),
        name="halo",
    )(act, volume[0])
    w = weight.reshape(3, 9 * ch, ch)
    w2 = jnp.concatenate([jnp.pad(w, ((0, 1), (0, 0), (0, 0))), jnp.pad(w, ((1, 0), (0, 0), (0, 0)))],
                         axis=-1).reshape(36 * ch, 2 * ch)
    bias2 = jnp.concatenate([bias, bias])[None]
    rows = ny * nz
    out, g = pl.pallas_call(
        functools.partial(work_kernel, nz, edge),
        out_shape=(jax.ShapeDtypeStruct((nx, rows, ch), BF),
                   jax.ShapeDtypeStruct((28, ch, ch), F32)),
        in_specs=[SM] + [VM] * 6, out_specs=(VM, VM),
        scratch_shapes=[pltpu.VMEM((nx + 2, rows + 2 * nz, 3 * ch), BF),
                        pltpu.VMEM(((nx + 4) * ch, rows), BF),
                        pltpu.VMEM((3 * ch, 9 * ch), F32)],
        compiler_params=big, name="work",
    )(act, volume.reshape(nx, rows, ch), hx.reshape(2, rows, ch), hy, w2, bias2,
      cotangent.reshape(nx, rows, ch))
    sh = 28 * ch // 32
    chunks = ((0, 48), (48, 32), (80, 32))
    total = pl.pallas_call(
        functools.partial(reduce_kernel, nsx, chunks),
        out_shape=jax.ShapeDtypeStruct((2, 4, 4, sh, ch), F32),
        in_specs=[VM], out_specs=VM,
        scratch_shapes=[pltpu.VMEM((16, sh, ch), BF), pltpu.VMEM((16, sh, ch), BF),
                        pltpu.VMEM((4, 4, sh, ch), F32), pltpu.VMEM((4, 4, sh, ch), BF),
                        pltpu.VMEM((4, 4, sh, ch), BF), pltpu.VMEM((4, sh, ch), F32),
                        pltpu.VMEM((4, sh, ch), BF), pltpu.VMEM((4, sh, ch), BF),
                        pltpu.VMEM((max(nsx // 2, 1), sh, ch), BF),
                        pltpu.VMEM((2, 4, 4, sh, ch), BF),
                        pltpu.SemaphoreType.DMA((len(chunks), 13 + max(nsx // 2, 1))),
                        pltpu.SemaphoreType.DMA((len(chunks), 13 + max(nsx // 2, 1)))],
        compiler_params=pltpu.CompilerParams(collective_id=1, has_side_effects=True,
                                             vmem_limit_bytes=32 * 2**20),
        name="reduce",
    )(g.reshape(2, 16, sh, ch)).reshape(28, ch, ch)
    return (out.reshape(volume.shape), total[:27].reshape(weight.shape), total[27, 0])


def solution(mesh):
    tile = P("dp", "sx", "sy", None, None)
    return jax.shard_map(
        functools.partial(local, mesh.shape["sx"], mesh.shape["sy"]),
        mesh=mesh,
        in_specs=(tile, P("dp", "sx", "sy", None), P(), P(), tile),
        out_specs=(tile, P(), P()),
        check_vma=False,
    )
```

time: 239 us -> 81.5 us (0.34); the launches traced: 235 us -> 81.3 us
  waiting for transfers between devices: 97.8 us -> 0 us
  Pallas kernels: 0 us -> 70.6 us
  matrix products: 49.7 us -> 0 us
  blocking collectives: 39.7 us -> 0 us
  between operations: 14.6 us -> 0.66 us
  starting transfers between devices: 11 us -> 0 us
  local copies, waits for them, and re-layouts: 15.3 us -> 7.07 us
  other arithmetic: 7.05 us -> 2.96 us
    psum x1 -> x0, waiting for transfers between devices: 86.5 us -> none  [local(): grad_w, grad_b = lax.psum((grad_w, grad_b), ('dp', 'sx', 'sy'))]
    pallas_call x0 -> x3, Pallas kernels: none -> 70.6 us  [the longest x1 32.9 us: local(): pl.pallas_call(functools.partial(work_kernel, nz, edge), out_shape=(jax.S...]
    psum x1 -> x0, blocking collectives: 39.7 us -> none  [local(): grad_w, grad_b = lax.psum((grad_w, grad_b), ('dp', 'sx', 'sy'))]
    dot_general x27 -> x0, matrix products: 27.4 us -> none  [layer_work(): lax.dot_general(piece, dpre, (((0, 1, 2, 3), (0, 1, 2, 3)), ((), ())), pr...]
    conv_general_dilated x1 -> x0, matrix products: 22.2 us -> none  [layer_work(): lax.conv_general_dilated(slab, weight, (1, 1, 1), 'VALID', dimension_numb...]
    ppermute x4 -> x0, waiting for transfers between devices: 11.3 us -> none  [the longest x2 8.52 us: with_halo(): lax.ppermute(lax.slice_in_dim(block, 0, width, axis=dim), axis, backward)]
    ppermute x4 -> x0, starting transfers between devices: 11 us -> none  [the longest x2 8.37 us: with_halo(): lax.ppermute(lax.slice_in_dim(block, block.shape[dim] - width, None, axis...]
    mul x1 -> x0, local copies, waits for them, and re-layouts: 3.4 us -> none  [layer_work(): out = (pre * sig * vox_mask).astype(jnp.bfloat16)]
  transfers between devices with their start and end apart: 5 -> 0, of which waited for: 5 -> 0; matrix products, arithmetic and copies ran while one was open for 2% -> 0% of each run, Pallas kernels for 0% -> 0%
where the time goes in v1:
time: 81.5 us; the launch traced here: 81.3 us
  Pallas kernels  70.6 us (87%)
  local copies, waits for them, and re-layouts  7.07 us (9%)
  other arithmetic  2.96 us (4%)
    pallas_call x1, Pallas kernels, local(): pl.pallas_call(functools.partial(work_kernel, nz, edge), out_shape=(jax.S...  32.9 us
    pallas_call x1, Pallas kernels, local(): pl.pallas_call(functools.partial(reduce_kernel, nsx, chunks), out_shape=j...  28.2 us
    pallas_call x1, Pallas kernels, local(): pl.pallas_call(functools.partial(halo_kernel, nsx, nsy, edge), out_shape=...  9.6 us
    unnamed x12, local copies, waits for them, and re-layouts  5.16 us
    concatenate x1, other arithmetic, local(): jnp.concatenate([jnp.pad(w, ((0, 1), (0, 0), (0, 0))), jnp.pad(w, ((1, 0)...  1.64 us

profile of v1, /device:TPU:0, one launch (start us, length us, event | category | flops | bytes accessed | tf_op | source)
XLA Modules:
  0.0 81.3 jit_solution(9293788973187837883)
XLA Ops:
  0.6 1.3 %pad_maximum_fusion = f32[256]{0:T(256)} fusion(f32[128]{0:T(128)} %param.8), kind=kLoop, calls=%fused_computation.5 | loop fusion | flops 256 | bytes 1536 | tf_op jit(solution)/shard_map/concatenate | solution.py:317
  2.0 0.0 copy-start
  2.0 1.6 %copy-done = bf16[1,16,16,32,128]{4,3,2,1,0:T(8,128)(2,1)S(1)} copy-done((bf16[1,16,16,32,128]{4,3,2,1,0:T(8,128)(2,1)S(1)}, bf16[1,16,16,32,128]{4,3,2,1,0:T(8,128)(2,1)}, u32[]{:S(2)}) %copy-start) | copy-done | bytes 2097176
  3.5 0.0 copy-start.4
  3.6 0.7 copy-done.4
  4.2 0.0 copy-start.5
  4.2 9.6 %halo.1 = (bf16[2,16,32,128]{3,2,1,0:T(8,128)(2,1)S(1)}, bf16[2,18,32,128]{3,2,1,0:T(8,128)(2,1)S(1)}) custom-call(s32[2]{0:T(128)S(1)} %bitcast.21, bf16[16,16,32,128]{3,2,1,0:T(8,128)(2,1)S(1)} %bitcast.15), custom_call_target="tpu_custom_call" | custom-call | tf_op jit(solution)/shard_map/halo/pallas_call | solution.py:303
  13.8 0.0 copy-start.2
  13.8 0.7 copy-done.2
  14.5 0.0 copy-start.3
  14.5 0.7 copy-done.3
  15.2 0.0 copy-done.5
  15.2 1.6 %fusion.2 = bf16[4,1152,256]{2,1,0:T(8,128)(2,1)} fusion(bf16[3,1152,128]{2,1,0:T(8,128)(2,1)S(1)} %bitcast.25), kind=kLoop, calls=%fused_computation.4 | loop fusion | flops 9437184 | bytes 3244032 | tf_op jit(solution)/shard_map/concatenate | solution.py:315
  16.9 32.9 %work.1 = (bf16[16,512,128]{2,1,0:T(8,128)(2,1)}, f32[28,128,128]{2,1,0:T(8,128)}) custom-call(s32[2]{0:T(128)} %bitcast.20, bf16[16,512,128]{2,1,0:T(8,128)(2,1)} %bitcast.14, bf16[2,512,128]{2,1,0:T(8,128)(2,1)} %bitcast.19, bf16[2,18,32,128]{3,2,1,0:T(8,128)(2,1)} %copy-done.2, bf16[4608,256]{1,0:T(8,128)(2,1)} %bitcast.22, f32[1,256]{1,0:T(1,128)} %bitcast.26, ...), custom_call_target="tpu_custom_call" | custom-call | tf_op jit(solution)/shard_map/work/pallas_call | solution.py:319
  49.7 0.0 copy-start.1
  49.7 1.5 %copy-done.1 = f32[28,128,128]{2,1,0:T(8,128)S(1)} copy-done((f32[28,128,128]{2,1,0:T(8,128)S(1)}, f32[28,128,128]{2,1,0:T(8,128)}, u32[]{:S(2)}) %copy-start.1) | copy-done | bytes 1835032
  51.2 28.2 %reduce.1 = f32[2,4,4,112,128]{4,3,2,1,0:T(8,128)S(1)} custom-call(f32[2,16,112,128]{3,2,1,0:T(8,128)S(1)} %bitcast.18), custom_call_target="tpu_custom_call" | custom-call | tf_op jit(solution)/shard_map/reduce/pallas_call | solution.py:332
  79.4 0.5 slice_bitcast_fusion
  79.9 1.4 %slice.8 = f32[27,128,128]{2,1,0:T(8,128)} slice(f32[28,128,128]{2,1,0:T(8,128)S(1)} %bitcast.17), slice={[0:27], [0:128], [0:128]} | slice | bytes 3538944 | tf_op jit(solution)/shard_map/slice | solution.py:348
Async XLA Ops:
  2.0 1.6 %copy-start = (bf16[1,16,16,32,128]{4,3,2,1,0:T(8,128)(2,1)S(1)}, bf16[1,16,16,32,128]{4,3,2,1,0:T(8,128)(2,1)}, u32[]{:S(2)}) copy-start(bf16[1,16,16,32,128]{4,3,2,1,0:T(8,128)(2,1)} %param.5) | copy-start | bytes 6291460
  3.5 0.7 copy-start.4
  4.2 11.0 %copy-start.5 = (bf16[3,3,3,128,128]{4,3,2,1,0:T(8,128)(2,1)S(1)}, bf16[3,3,3,128,128]{4,3,2,1,0:T(8,128)(2,1)}, u32[]{:S(2)}) copy-start(bf16[3,3,3,128,128]{4,3,2,1,0:T(8,128)(2,1)} %param.7) | copy-start | bytes 2654212
  13.8 0.7 copy-start.2
  14.5 0.7 copy-start.3
  49.7 1.5 %copy-start.1 = (f32[28,128,128]{2,1,0:T(8,128)S(1)}, f32[28,128,128]{2,1,0:T(8,128)}, u32[]{:S(2)}) copy-start(f32[28,128,128]{2,1,0:T(8,128)} %get-tuple-element.10) | copy-start | bytes 5505028

commit v2 on v1

v2 whole, which is shorter than its diff:
```python
import functools

import jax
import jax.numpy as jnp
from jax import lax
from jax.experimental import pallas as pl
from jax.experimental.pallas import tpu as pltpu
from jax.sharding import PartitionSpec as P

MESH = pl.DeviceIdType.MESH
VM = pl.BlockSpec(memory_space=pltpu.VMEM)
SM = pl.BlockSpec(memory_space=pltpu.SMEM)
NEAR = [(dx, dy) for dx in (-1, 0, 1) for dy in (-1, 0, 1) if (dx, dy) != (0, 0)]
BF = jnp.bfloat16
F32 = jnp.float32


def depth_mask(act_ref, rows, depth, edge):
    z = lax.rem(lax.broadcasted_iota(jnp.int32, (rows, 128), 0), depth)
    m = jnp.zeros((rows, 128), F32)
    for k in range(depth // edge):
        inside = jnp.logical_and(z >= k * edge, z < (k + 1) * edge)
        m = jnp.where(inside, act_ref[k].astype(F32), m)
    return m


def layer_kernel(nsx, nsy, edge, chunks, act_ref, bias_ref, vol_ref, w_ref, cot_ref,
                 out_ref, gw_ref, gb_ref, fx, fy, hx, hy, vb, wb, cb, ob, cols, dpt, acc,
                 g_ref, s1, r1, a1, s2, r2, a2, s3, r3, s4, fin, ls, hs, hr, ss, rs):
    nx, ny, nz, ch = vol_ref.shape
    rows = ny * nz
    d, x, y = lax.axis_index("dp"), lax.axis_index("sx"), lax.axis_index("sy")

    def there(dx, dy):
        return (x + dx >= 0) & (x + dx < nsx) & (y + dy >= 0) & (y + dy < nsy)

    h, dh = lax.rem(d, 2), d // 2
    xl, xh = lax.rem(x, 2), x // 2
    q = dh * 2 + xl
    far = nsx // 2

    def peer1():
        return {"dp": dh * 2 + 1 - h, "sx": x, "sy": y}

    def peer2(k):
        o = lax.rem(q + k, 4)
        return o, {"dp": (o // 2) * 2 + h, "sx": xh * 2 + lax.rem(o, 2), "sy": y}

    def peer3(k):
        o = lax.rem(y + k, 4)
        return o, {"dp": d, "sx": x, "sy": o}

    def peer4(k):
        o = lax.rem(xh + k, far)
        return o, {"dp": d, "sx": o * 2 + xl, "sy": y}

    peers = [peer1()] + [peer2(k)[1] for k in (1, 2, 3)] + [peer3(k)[1] for k in (1, 2, 3)]
    peers += [peer4(k)[1] for k in range(1, far)]
    barrier = pltpu.get_barrier_semaphore()
    for p in peers:
        pl.semaphore_signal(barrier, inc=1, device_id=p, device_id_type=MESH)
    for dx, dy in NEAR:
        @pl.when(there(dx, dy))
        def _():
            pl.semaphore_signal(barrier, inc=1, device_id={"sx": x + dx, "sy": y + dy},
                                device_id_type=MESH)
    load = [pltpu.make_async_copy(s, t, ls.at[k]) for k, (s, t) in enumerate((
        (vol_ref.at[0], fx.at[0]), (vol_ref.at[nx - 1], fx.at[1]),
        (vol_ref.at[:, 0], fy.at[0]), (vol_ref.at[:, ny - 1], fy.at[1]),
        (vol_ref, vb), (w_ref, wb.at[pl.ds(0, 27 * ch), pl.ds(0, ch)]),
        (w_ref, wb.at[pl.ds(9 * ch, 27 * ch), pl.ds(ch, ch)]), (cot_ref, cb)))]
    for r in load:
        r.start()
    zmask = depth_mask(act_ref, nz, nz, edge)[None].astype(BF)
    mask = depth_mask(act_ref, rows, nz, edge)
    wb[0:9 * ch, ch:2 * ch] = jnp.zeros((9 * ch, ch), BF)
    wb[27 * ch:36 * ch, 0:ch] = jnp.zeros((9 * ch, ch), BF)
    dpt[0:2 * ch, :] = jnp.zeros((2 * ch, rows), BF)
    dpt[(nx + 2) * ch:(nx + 4) * ch, :] = jnp.zeros((2 * ch, rows), BF)
    for r in load[:4]:
        r.wait()
    for side in range(2):
        fx[side] = fx[side] * zmask
        fy[side] = fy[side] * zmask
    pl.semaphore_wait(barrier, len(peers) + sum(there(dx, dy).astype(jnp.int32) for dx, dy in NEAR))

    def slot(dx, dy):
        if dy == 0:
            return hx.at[int(dx > 0)]
        if dx == 0:
            return hy.at[int(dy > 0), pl.ds(1, nx)]
        return hy.at[int(dy > 0), (nx + 1) * int(dx > 0)]

    def face(k):
        dx, dy = NEAR[k]
        if dy == 0:
            src = fx.at[int(dx > 0)]
        elif dx == 0:
            src = fy.at[int(dy > 0)]
        else:
            src = fx.at[int(dx > 0), (ny - 1) * int(dy > 0)]
        opp = NEAR.index((-dx, -dy))
        return pltpu.make_async_remote_copy(
            src_ref=src, dst_ref=slot(-dx, -dy), send_sem=hs.at[k], recv_sem=hr.at[opp],
            device_id={"sx": x + dx, "sy": y + dy}, device_id_type=MESH)

    for k, (dx, dy) in enumerate(NEAR):
        @pl.when(there(dx, dy))
        def _():
            face(k).start()

        @pl.when(jnp.logical_not(there(dx, dy)))
        def _():
            ref = slot(dx, dy)
            ref[...] = jnp.zeros(ref.shape, BF)

    z = lax.rem(lax.broadcasted_iota(jnp.int32, (rows, ch), 0), nz)
    first, last = z == 0, z == nz - 1

    def shifted(i, at, v):
        n = v.shape[0]
        here = pl.ds(at, n)
        cols[i, here, ch:2 * ch] = v.astype(BF)
        cols[i, here, 0:ch] = jnp.where(first[:n], 0.0, pltpu.roll(v, 1, 0)).astype(BF)
        cols[i, here, 2 * ch:3 * ch] = jnp.where(last[:n], 0.0, pltpu.roll(v, n - 1, 0)).astype(BF)

    load[4].wait()

    @pl.loop(0, nx)
    def _(i):
        shifted(i + 1, nz, vb[i].reshape(rows, ch).astype(F32) * mask)

    for k, (dx, dy) in enumerate(NEAR):
        @pl.when(there(dx, dy))
        def _():
            face(k).wait_send()
            face(NEAR.index((-dx, -dy))).wait_recv()
    for side in range(2):
        shifted(side * (nx + 1), nz, hx[side].reshape(rows, ch).astype(F32))

    @pl.loop(0, nx + 2)
    def _(i):
        for side in range(2):
            shifted(i, side * (nz + rows), hy[side, i].astype(F32))

    for r in load[5:]:
        r.wait()
    half = 18 * ch

    def pair(p, gb):
        pre = jnp.zeros((rows, 2 * ch), F32) + bias_ref[...]
        for j in range(2):
            lhs = jnp.concatenate(
                [cols[2 * p + 2 * j + t, pl.ds(b * nz, rows), :] for t in range(2) for b in range(3)], axis=1)
            pre = pre + jnp.dot(lhs, wb[j * half:(j + 1) * half, :], preferred_element_type=F32)
        for t in range(2):
            u = pre[:, t * ch:(t + 1) * ch]
            sig = jax.nn.sigmoid(u)
            ob[2 * p + t] = (u * sig * mask).astype(BF)
            e = (cb[2 * p + t].astype(F32) * sig * (1.0 + u * (1.0 - sig)) * mask).astype(BF)
            gb = gb + jnp.sum(e.astype(F32), axis=0, keepdims=True)
            dpt[pl.ds(pl.multiple_of((2 * p + t + 2) * ch, ch), ch), :] = e.T
        return gb

    gb = lax.fori_loop(0, nx // 2, pair, jnp.zeros((1, ch), F32))
    store = pltpu.make_async_copy(ob, out_ref, ls.at[8])
    store.start()

    def grad(q0, q1, i0, i1):
        @pl.loop(i0, i1)
        def _(p):
            i = 2 * p
            lhs = jnp.concatenate(
                [dpt[pl.ds(pl.multiple_of((i + t) * ch, ch), 3 * ch), :] for t in range(2)], axis=1)
            rhs = jnp.concatenate([jnp.concatenate(
                [cols[i + t, pl.ds((o // 3) * nz, rows), (o % 3) * ch:(o % 3 + 1) * ch] for o in range(q0, q1)],
                axis=1) for t in range(2)], axis=0)
            acc[:, q0 * ch:q1 * ch] += jnp.dot(lhs, rhs, preferred_element_type=F32)

    def put(pos, tile):
        g_ref[pos % 4 // 2, pl.ds(8 * (pos % 2), 8), pos // 4] = tile.reshape(8, 16, ch)

    def tiles(q0, q1):
        for o in range(q0, q1):
            for a in range(3):
                put(o * 3 + a, acc[(2 - a) * ch:(3 - a) * ch, o * ch:(o + 1) * ch].T)

    def rcopy(src, dst, c, n, p):
        return pltpu.make_async_remote_copy(src_ref=src, dst_ref=dst, send_sem=ss.at[c, n],
                                            recv_sem=rs.at[c, n], device_id=p, device_id_type=MESH)

    def part(c):
        off, size = chunks[c]
        return pl.ds(off, size)

    def c1(c):
        return [rcopy(s1.at[:, part(c)], r1.at[:, part(c)], c, 0, peer1())]

    def c2(c):
        cs = []
        for k in (1, 2, 3):
            o, p = peer2(k)
            cs.append(rcopy(s2.at[o, :, part(c)], r2.at[k, :, part(c)], c, k, p))
        return cs

    def c3(c):
        cs = []
        for k in (1, 2, 3):
            o, p = peer3(k)
            cs.append(rcopy(s3.at[o, part(c)], r3.at[k, part(c)], c, 3 + k, p))
        return cs

    def c4(c):
        cs = []
        for k in range(1, far):
            o, p = peer4(k)
            cs.append(rcopy(s4.at[xh, part(c)], s4.at[xh, part(c)], c, 13 + k, p))
        return cs

    def c4in(c):
        cs = []
        for k in range(1, far):
            o, p = peer4(far - k)
            cs.append(rcopy(s4.at[xh, part(c)], s4.at[o, part(c)], c, 13 + k, p))
        return cs

    def g3(c, inn=False):
        cs = []
        for k in (1, 2, 3):
            o, p = peer3(4 - k if inn else k)
            cs.append(rcopy(fin.at[h, q, y, part(c)], fin.at[h, q, o if inn else y, part(c)], c, 6 + k, p))
        return cs

    def g2(c, inn=False):
        cs = []
        for k in (1, 2, 3):
            o, p = peer2(4 - k if inn else k)
            cs.append(rcopy(fin.at[h, q, :, part(c)], fin.at[h, o if inn else q, :, part(c)], c, 9 + k, p))
        return cs

    def g1(c, inn=False):
        return [rcopy(fin.at[h, :, :, part(c)], fin.at[1 - h if inn else h, :, :, part(c)], c, 13, peer1())]

    def start(cs):
        for r in cs:
            r.start()

    def landed(cs):
        for r in cs:
            r.wait_recv()

    def st0(c):
        s1[:, part(c)] = g_ref[1 - h, :, part(c)].astype(BF)
        start(c1(c))

    def st1(c):
        landed(c1(c))
        v = g_ref[h, :, part(c)] + r1[:, part(c)].astype(F32)
        v = v.reshape((4, 4) + v.shape[1:])
        a1[:, :, part(c)] = v
        s2[:, :, part(c)] = v.astype(BF)
        start(c2(c))

    def st2(c):
        landed(c2(c))
        v = a1[q, :, part(c)]
        for k in (1, 2, 3):
            v = v + r2[k, :, part(c)].astype(F32)
        a2[:, part(c)] = v
        s3[:, part(c)] = v.astype(BF)
        start(c3(c))

    def st3(c):
        landed(c3(c))
        v = a2[y, part(c)]
        for k in (1, 2, 3):
            v = v + r3[k, part(c)].astype(F32)
        if far > 1:
            s4[xh, part(c)] = v.astype(BF)
            start(c4(c))
            landed(c4in(c))
            v = s4[0, part(c)].astype(F32)
            for k in range(1, far):
                v = v + s4[k, part(c)].astype(F32)
        fin[h, q, y, part(c)] = v.astype(BF)
        start(g3(c))

    def st4(c):
        landed(g3(c, True))
        start(g2(c))

    def st5(c):
        landed(g2(c, True))
        start(g1(c))

    def st6(c):
        landed(g1(c, True))
        off, size = chunks[c]
        for pos in range(4 * off, 4 * (off + size)):
            k = pos % 4
            tile = fin[k // 2, 2 * (k % 2):2 * (k % 2) + 2, :, pos // 4].reshape(ch, ch)
            if pos < 27:
                gw_ref[(pos % 3) * 9 + pos // 3] = tile
            else:
                gb_ref[...] = tile[0:16]

    st = [st0, st1, st2, st3, st4, st5, st6]
    acc[...] = jnp.zeros(acc.shape, F32)
    n = (nx + 2) // 2
    m = n // 2
    put(27, jnp.broadcast_to(gb, (ch, ch)))
    grad(0, 4, 0, n)
    tiles(0, 4)
    st[0](0)
    grad(4, 7, 0, m)
    st[1](0)
    grad(4, 7, m, n)
    tiles(4, 7)
    st[0](1)
    grad(7, 9, 0, m)
    st[2](0)
    st[1](1)
    grad(7, 9, m, n)
    tiles(7, 9)
    st[0](2)
    for s, c in ((3, 0), (2, 1), (1, 2), (4, 0), (3, 1), (5, 0), (2, 2), (4, 1), (6, 0), (5, 1), (3, 2),
                 (6, 1), (4, 2), (5, 2), (6, 2)):
        st[s](c)
    store.wait()
    for c in range(len(chunks)):
        for cs in (c1(c), c2(c), c3(c), c4(c), g3(c), g2(c), g1(c)):
            for r in cs:
                r.wait_send()


def local(nsx, nsy, volume, block_active, weight, bias, cotangent):
    _, nx, ny, nz, ch = volume.shape
    blocks = block_active.shape[3]
    rows = ny * nz
    chunks = ((0, 3), (3, 2), (5, 2))
    far = max(nsx // 2, 1)
    anyw = pl.BlockSpec(memory_space=pl.ANY)
    gr = (7, 16, ch)
    bf = lambda *dims: pltpu.VMEM(dims, BF)
    dma = pltpu.SemaphoreType.DMA
    out, gw, gb = pl.pallas_call(
        functools.partial(layer_kernel, nsx, nsy, nz // blocks, chunks),
        out_shape=(jax.ShapeDtypeStruct((nx, rows, ch), BF),
                   jax.ShapeDtypeStruct((27, ch, ch), BF),
                   jax.ShapeDtypeStruct((16, ch), BF)),
        in_specs=[SM, VM, anyw, anyw, anyw], out_specs=(anyw, VM, VM),
        scratch_shapes=[
            bf(2, ny, nz, ch), bf(2, nx, nz, ch), bf(2, ny, nz, ch), bf(2, nx + 2, nz, ch),
            bf(nx, ny, nz, ch), bf(36 * ch, 2 * ch), bf(nx, rows, ch), bf(nx, rows, ch),
            bf(nx + 2, rows + 2 * nz, 3 * ch), bf((nx + 4) * ch, rows), pltpu.VMEM((3 * ch, 9 * ch), F32),
            pltpu.VMEM((2, 16) + gr, F32), bf(16, *gr), bf(16, *gr), pltpu.VMEM((4, 4) + gr, F32),
            bf(4, 4, *gr), bf(4, 4, *gr), pltpu.VMEM((4,) + gr, F32), bf(4, *gr), bf(4, *gr),
            bf(far, *gr), bf(2, 4, 4, *gr), dma((9,)), dma((8,)), dma((8,)),
            dma((len(chunks), 13 + far)), dma((len(chunks), 13 + far))],
        compiler_params=pltpu.CompilerParams(collective_id=0, has_side_effects=True,
                                             vmem_limit_bytes=60 * 2**20),
        name="layer",
    )(block_active.reshape(blocks), jnp.concatenate([bias, bias])[None], volume[0],
      weight.reshape(27 * ch, ch), cotangent.reshape(nx, rows, ch))
    return (out.reshape(volume.shape), gw.reshape(weight.shape).astype(F32), gb[0].astype(F32))


def solution(mesh):
    tile = P("dp", "sx", "sy", None, None)
    return jax.shard_map(
        functools.partial(local, mesh.shape["sx"], mesh.shape["sy"]),
        mesh=mesh,
        in_specs=(tile, P("dp", "sx", "sy", None), P(), P(), tile),
        out_specs=(tile, P(), P()),
        check_vma=False,
    )
```

time: 81.5 us -> 69.8 us (0.86)
  Pallas kernels: 70.6 us -> 62.5 us
  local copies, waits for them, and re-layouts: 7.07 us -> 1.32 us
  other arithmetic: 2.96 us -> 5.2 us
    pallas_call x3 -> x1, Pallas kernels: 70.6 us -> 62.5 us  [local(): pl.pallas_call(functools.partial(layer_kernel, nsx, nsy, nz // blocks, ch...]
    convert_element_type x0 -> x2, other arithmetic: none -> 3.9 us  [the longest x1 2.58 us: local(): gw.reshape(weight.shape).astype(F32)]
    unnamed x12 -> x3, local copies, waits for them, and re-layouts: 5.16 us -> 1.32 us
    concatenate x2 -> x1, other arithmetic: 2.96 us -> 1.3 us  [local(): jnp.concatenate([bias, bias])[None]]
    slice x1 -> x0, local copies, waits for them, and re-layouts: 1.4 us -> none  [local(): total[:27].reshape(weight.shape)]
where the time goes in v2:
time: 69.8 us; the launch traced here: 69.6 us
  Pallas kernels  62.5 us (90%)
  other arithmetic  5.2 us (7%)
  local copies, waits for them, and re-layouts  1.32 us (2%)
    pallas_call x1, Pallas kernels, local(): pl.pallas_call(functools.partial(layer_kernel, nsx, nsy, nz // blocks, ch...  62.5 us
    convert_element_type x1, other arithmetic, local(): gw.reshape(weight.shape).astype(F32)  2.58 us

profile of v2, /device:TPU:0, one launch (start us, length us, event | category | flops | bytes accessed | tf_op | source)
XLA Modules:
  0.0 69.6 jit_solution(12050134624560459985)
XLA Ops:
  0.6 1.3 %pad_maximum_fusion = f32[256]{0:T(256)} fusion(f32[128]{0:T(128)} %param.8), kind=kLoop, calls=%fused_computation | loop fusion | flops 256 | bytes 1536 | tf_op jit(solution)/shard_map/concatenate | solution.py:363
  1.9 62.5 %layer.1 = (bf16[16,512,128]{2,1,0:T(8,128)(2,1)}, bf16[27,128,128]{2,1,0:T(8,128)(2,1)}, bf16[16,128]{1,0:T(8,128)(2,1)}) custom-call(s32[2]{0:T(128)} %bitcast.17, f32[1,256]{1,0:T(1,128)} %bitcast.16, bf16[16,16,32,128]{3,2,1,0:T(8,128)(2,1)} %bitcast.11, bf16[3456,128]{1,0:T(8,128)(2,1)} %bitcast.15, bf16[16,512,128]{2,1,0:T(8,128)(2,1)} %bitcast.12), custom_call_target="tpu_custom_call" | custom-call | tf_op jit(solution)/shard_map/layer/pallas_call | solution.py:346
  64.4 0.0 copy-start
  64.4 1.3 %bitcast_convert_fusion = f32[128]{0:T(128)} fusion(bf16[16,128]{1,0:T(8,128)(2,1)} %get-tuple-element.8), kind=kLoop, calls=%fused_computation.1 | loop fusion | flops 128 | bytes 768 | tf_op jit(solution)/shard_map/convert_element_type | solution.py:365
  65.7 2.6 %convert.2 = f32[3,3,3,128,128]{4,3,2,1,0:T(8,128)} convert(bf16[3,3,3,128,128]{4,3,2,1,0:T(8,128)(2,1)} %bitcast.14) | non-fusion elementwise | flops 442368 | bytes 2654208 | tf_op jit(solution)/shard_map/convert_element_type | solution.py:365
  68.3 0.0 copy-done
  68.3 1.3 %copy.9 = bf16[1,16,16,32,128]{4,3,2,1,0:T(8,128)(2,1)} copy(bf16[1,16,16,32,128]{4,3,2,1,0:T(8,128)(2,1)S(1)} %bitcast.13) | data formatting | bytes 4194304
Async XLA Ops:
  64.4 3.9 %copy-start = (bf16[16,512,128]{2,1,0:T(8,128)(2,1)S(1)}, bf16[16,512,128]{2,1,0:T(8,128)(2,1)}, u32[]{:S(2)}) copy-start(bf16[16,512,128]{2,1,0:T(8,128)(2,1)} %get-tuple-element.6) | copy-start | bytes 6291460

commit v3 on v2

--- a/solution.py
+++ b/solution.py
@@ -25,7 +25,7 @@
 
 
 def layer_kernel(nsx, nsy, edge, chunks, act_ref, bias_ref, vol_ref, w_ref, cot_ref,
-                 out_ref, gw_ref, gb_ref, fx, fy, hx, hy, vb, wb, cb, ob, cols, dpt, acc,
+                 out_ref, gw_ref, gb_ref, fx, fy, hx, hy, vb, wb, cb, ob, cols, dpt, acc, prea, preb,
                  g_ref, s1, r1, a1, s2, r2, a2, s3, r3, s4, fin, ls, hs, hr, ss, rs):
     nx, ny, nz, ch = vol_ref.shape
     rows = ny * nz
@@ -147,22 +147,38 @@
         r.wait()
     half = 18 * ch
 
-    def pair(p, gb):
-        pre = jnp.zeros((rows, 2 * ch), F32) + bias_ref[...]
+    bias2 = jnp.concatenate([bias_ref[...], bias_ref[...]], axis=1)
+
+    def conv(p, into):
+        pre = jnp.zeros((rows, 2 * ch), F32) + bias2
         for j in range(2):
             lhs = jnp.concatenate(
                 [cols[2 * p + 2 * j + t, pl.ds(b * nz, rows), :] for t in range(2) for b in range(3)], axis=1)
             pre = pre + jnp.dot(lhs, wb[j * half:(j + 1) * half, :], preferred_element_type=F32)
+        into[...] = pre
+
+    def finish(p, pre, gb):
         for t in range(2):
             u = pre[:, t * ch:(t + 1) * ch]
             sig = jax.nn.sigmoid(u)
             ob[2 * p + t] = (u * sig * mask).astype(BF)
             e = (cb[2 * p + t].astype(F32) * sig * (1.0 + u * (1.0 - sig)) * mask).astype(BF)
             gb = gb + jnp.sum(e.astype(F32), axis=0, keepdims=True)
-            dpt[pl.ds(pl.multiple_of((2 * p + t + 2) * ch, ch), ch), :] = e.T
+            at = (2 * p + t + 2) * ch
+            dpt[pl.ds(at if isinstance(at, int) else pl.multiple_of(at, ch), ch), :] = e.T
         return gb
 
-    gb = lax.fori_loop(0, nx // 2, pair, jnp.zeros((1, ch), F32))
+    def pairs(k, gb):
+        conv(2 * k + 1, preb)
+        gb = finish(2 * k, prea, gb)
+        conv(2 * k + 2, prea)
+        return finish(2 * k + 1, preb, gb)
+
+    conv(0, prea)
+    gb = lax.fori_loop(0, nx // 4 - 1, pairs, jnp.zeros((1, ch), F32))
+    conv(nx // 2 - 1, preb)
+    gb = finish(nx // 2 - 2, prea, gb)
+    gb = finish(nx // 2 - 1, preb, gb)
     store = pltpu.make_async_copy(ob, out_ref, ls.at[8])
     store.start()
 
@@ -300,32 +316,30 @@
             k = pos % 4
             tile = fin[k // 2, 2 * (k % 2):2 * (k % 2) + 2, :, pos // 4].reshape(ch, ch)
             if pos < 27:
-                gw_ref[(pos % 3) * 9 + pos // 3] = tile
+                gw_ref[(pos % 3) * 9 + pos // 3] = tile.astype(F32)
             else:
-                gb_ref[...] = tile[0:16]
+                gb_ref[...] = tile[0:16].astype(F32)[0:1]
 
     st = [st0, st1, st2, st3, st4, st5, st6]
     acc[...] = jnp.zeros(acc.shape, F32)
     n = (nx + 2) // 2
-    m = n // 2
     put(27, jnp.broadcast_to(gb, (ch, ch)))
-    grad(0, 4, 0, n)
-    tiles(0, 4)
-    st[0](0)
-    grad(4, 7, 0, m)
-    st[1](0)
-    grad(4, 7, m, n)
-    tiles(4, 7)
-    st[0](1)
-    grad(7, 9, 0, m)
-    st[2](0)
-    st[1](1)
-    grad(7, 9, m, n)
-    tiles(7, 9)
-    st[0](2)
-    for s, c in ((3, 0), (2, 1), (1, 2), (4, 0), (3, 1), (5, 0), (2, 2), (4, 1), (6, 0), (5, 1), (3, 2),
-                 (6, 1), (4, 2), (5, 2), (6, 2)):
-        st[s](c)
+    ready = {0: (0,), 1: (1, 2), 2: (3,), 3: (4, 5), 4: (6,)}
+    at = {}
+    step = 0
+    while step < 5 or any(v < 7 for v in at.values()):
+        if step < 5:
+            q0, q1 = 2 * step, min(2 * step + 2, 9)
+            grad(q0, q1, 0, n)
+            tiles(q0, q1)
+        for c in sorted(at):
+            if at[c] < 7:
+                st[at[c]](c)
+                at[c] += 1
+        for c in ready.get(step, ()):
+            st[0](c)
+            at[c] = 1
+        step += 1
     store.wait()
     for c in range(len(chunks)):
         for cs in (c1(c), c2(c), c3(c), c4(c), g3(c), g2(c), g1(c)):
@@ -337,7 +351,7 @@
     _, nx, ny, nz, ch = volume.shape
     blocks = block_active.shape[3]
     rows = ny * nz
-    chunks = ((0, 3), (3, 2), (5, 2))
+    chunks = tuple((k, 1) for k in range(7))
     far = max(nsx // 2, 1)
     anyw = pl.BlockSpec(memory_space=pl.ANY)
     gr = (7, 16, ch)
@@ -346,13 +360,14 @@
     out, gw, gb = pl.pallas_call(
         functools.partial(layer_kernel, nsx, nsy, nz // blocks, chunks),
         out_shape=(jax.ShapeDtypeStruct((nx, rows, ch), BF),
-                   jax.ShapeDtypeStruct((27, ch, ch), BF),
-                   jax.ShapeDtypeStruct((16, ch), BF)),
+                   jax.ShapeDtypeStruct((27, ch, ch), F32),
+                   jax.ShapeDtypeStruct((1, ch), F32)),
         in_specs=[SM, VM, anyw, anyw, anyw], out_specs=(anyw, VM, VM),
         scratch_shapes=[
             bf(2, ny, nz, ch), bf(2, nx, nz, ch), bf(2, ny, nz, ch), bf(2, nx + 2, nz, ch),
             bf(nx, ny, nz, ch), bf(36 * ch, 2 * ch), bf(nx, rows, ch), bf(nx, rows, ch),
             bf(nx + 2, rows + 2 * nz, 3 * ch), bf((nx + 4) * ch, rows), pltpu.VMEM((3 * ch, 9 * ch), F32),
+            pltpu.VMEM((rows, 2 * ch), F32), pltpu.VMEM((rows, 2 * ch), F32),
             pltpu.VMEM((2, 16) + gr, F32), bf(16, *gr), bf(16, *gr), pltpu.VMEM((4, 4) + gr, F32),
             bf(4, 4, *gr), bf(4, 4, *gr), pltpu.VMEM((4,) + gr, F32), bf(4, *gr), bf(4, *gr),
             bf(far, *gr), bf(2, 4, 4, *gr), dma((9,)), dma((8,)), dma((8,)),
@@ -360,9 +375,9 @@
         compiler_params=pltpu.CompilerParams(collective_id=0, has_side_effects=True,
                                              vmem_limit_bytes=60 * 2**20),
         name="layer",
-    )(block_active.reshape(blocks), jnp.concatenate([bias, bias])[None], volume[0],
+    )(block_active.reshape(blocks), bias[None], volume[0],
       weight.reshape(27 * ch, ch), cotangent.reshape(nx, rows, ch))
-    return (out.reshape(volume.shape), gw.reshape(weight.shape).astype(F32), gb[0].astype(F32))
+    return (out.reshape(volume.shape), gw.reshape(weight.shape), gb.reshape(ch))
 
 
 def solution(mesh):

time: 69.8 us -> 70.1 us (level)
  other arithmetic: 5.2 us -> 0 us
  local copies, waits for them, and re-layouts: 1.32 us -> 5.23 us
  Pallas kernels: 62.5 us -> 64 us
    unnamed x3 -> x7, local copies, waits for them, and re-layouts: 1.32 us -> 5.23 us
    convert_element_type x2 -> x0, other arithmetic: 3.9 us -> none  [the longest x1 2.58 us: local(): gw.reshape(weight.shape).astype(F32)]
    pallas_call x1, Pallas kernels: 62.5 us -> 64 us  [local(): pl.pallas_call(functools.partial(layer_kernel, nsx, nsy, nz // blocks, ch...]
    concatenate x1 -> x0, other arithmetic: 1.3 us -> none  [local(): jnp.concatenate([bias, bias])[None]]
where the time goes in v3:
time: 70.1 us; the launch traced here: 69.9 us
  Pallas kernels  64 us (91%)
  local copies, waits for them, and re-layouts  5.23 us (7%)
    pallas_call x1, Pallas kernels, local(): pl.pallas_call(functools.partial(layer_kernel, nsx, nsy, nz // blocks, ch...  64 us
    unnamed x7, local copies, waits for them, and re-layouts  5.23 us

profile of v3, /device:TPU:0, one launch (start us, length us, event | category | flops | bytes accessed | tf_op | source)
XLA Modules:
  0.0 69.9 jit_solution(9090789503662516052)
XLA Ops:
  0.6 64.0 %layer.1 = (bf16[16,512,128]{2,1,0:T(8,128)(2,1)}, f32[27,128,128]{2,1,0:T(8,128)}, f32[1,128]{1,0:T(1,128)}) custom-call(s32[2]{0:T(128)} %bitcast.13, f32[1,128]{1,0:T(1,128)} %bitcast.14, bf16[16,16,32,128]{3,2,1,0:T(8,128)(2,1)} %bitcast.8, bf16[3456,128]{1,0:T(8,128)(2,1)} %bitcast.12, bf16[16,512,128]{2,1,0:T(8,128)(2,1)} %bitcast.9), custom_call_target="tpu_custom_call" | custom-call | tf_op jit(solution)/shard_map/layer/pallas_call | solution.py:360
  64.7 0.0 copy-start
  64.7 3.5 %copy.11 = bf16[1,16,16,32,128]{4,3,2,1,0:T(8,128)(2,1)} copy(bf16[1,16,16,32,128]{4,3,2,1,0:T(8,128)(2,1)} %bitcast.10) | data formatting | bytes 4194304
  68.2 0.0 copy-done
  68.2 0.0 copy-start.1
  68.2 1.2 %copy.12 = f32[3,3,3,128,128]{4,3,2,1,0:T(8,128)} copy(f32[3,3,3,128,128]{4,3,2,1,0:T(8,128)S(1)} %bitcast.11) | data formatting | bytes 3538944
  69.4 0.0 copy-done.1
  69.4 0.5 copy.13
Async XLA Ops:
  64.7 3.5 %copy-start = (f32[27,128,128]{2,1,0:T(8,128)S(1)}, f32[27,128,128]{2,1,0:T(8,128)}, u32[]{:S(2)}) copy-start(f32[27,128,128]{2,1,0:T(8,128)} %get-tuple-element.7) | copy-start | bytes 5308420
  68.2 1.2 %copy-start.1 = (f32[1,128]{1,0:T(1,128)S(1)}, f32[1,128]{1,0:T(1,128)}, u32[]{:S(2)}) copy-start(f32[1,128]{1,0:T(1,128)} %get-tuple-element.8) | copy-start | bytes 1540

commit v4 on v3

--- a/solution.py
+++ b/solution.py
@@ -25,8 +25,8 @@
 
 
 def layer_kernel(nsx, nsy, edge, chunks, act_ref, bias_ref, vol_ref, w_ref, cot_ref,
-                 out_ref, gw_ref, gb_ref, fx, fy, hx, hy, vb, wb, cb, ob, cols, dpt, acc, prea, preb,
-                 g_ref, s1, r1, a1, s2, r2, a2, s3, r3, s4, fin, ls, hs, hr, ss, rs):
+                 out_ref, gw_ref, fx, fy, hx, hy, vb, wb, cb, ob, cols, dpt, acc, prea, preb,
+                 g_ref, s1, r1, a1, s2, r2, a2, s3, r3, s4, s8, r8, fin, ls, hs, hr, ss, rs):
     nx, ny, nz, ch = vol_ref.shape
     rows = ny * nz
     d, x, y = lax.axis_index("dp"), lax.axis_index("sx"), lax.axis_index("sy")
@@ -54,7 +54,12 @@
         o = lax.rem(xh + k, far)
         return o, {"dp": d, "sx": o * 2 + xl, "sy": y}
 
-    peers = [peer1()] + [peer2(k)[1] for k in (1, 2, 3)] + [peer3(k)[1] for k in (1, 2, 3)]
+    def peer8(k):
+        o = lax.rem(h * 4 + q + k, 8)
+        oq = lax.rem(o, 4)
+        return o // 4, oq, {"dp": (oq // 2) * 2 + o // 4, "sx": xh * 2 + lax.rem(oq, 2), "sy": y}
+
+    peers = [peer8(k)[2] for k in range(1, 8)] + [peer3(k)[1] for k in (1, 2, 3)]
     peers += [peer4(k)[1] for k in range(1, far)]
     barrier = pltpu.get_barrier_semaphore()
     for p in peers:
@@ -194,7 +199,7 @@
             acc[:, q0 * ch:q1 * ch] += jnp.dot(lhs, rhs, preferred_element_type=F32)
 
     def put(pos, tile):
-        g_ref[pos % 4 // 2, pl.ds(8 * (pos % 2), 8), pos // 4] = tile.reshape(8, 16, ch)
+        g_ref[pos // 4, pos % 4 // 2, pl.ds(2 * (pos % 2), 2)] = tile.reshape(2, 4, 16, ch)
 
     def tiles(q0, q1):
         for o in range(q0, q1):
@@ -210,52 +215,43 @@
         return pl.ds(off, size)
 
     def c1(c):
-        return [rcopy(s1.at[:, part(c)], r1.at[:, part(c)], c, 0, peer1())]
+        return [rcopy(s1.at[part(c)], r1.at[part(c)], c, 0, peer1())]
 
     def c2(c):
-        cs = []
-        for k in (1, 2, 3):
-            o, p = peer2(k)
-            cs.append(rcopy(s2.at[o, :, part(c)], r2.at[k, :, part(c)], c, k, p))
-        return cs
+        return [rcopy(s2.at[part(c), o], r2.at[part(c), k], c, k, p)
+                for k in (1, 2, 3) for o, p in [peer2(k)]]
 
     def c3(c):
-        cs = []
-        for k in (1, 2, 3):
-            o, p = peer3(k)
-            cs.append(rcopy(s3.at[o, part(c)], r3.at[k, part(c)], c, 3 + k, p))
-        return cs
+        return [rcopy(s3.at[part(c), o], r3.at[part(c), k], c, 3 + k, p)
+                for k in (1, 2, 3) for o, p in [peer3(k)]]
 
     def c4(c):
-        cs = []
-        for k in range(1, far):
-            o, p = peer4(k)
-            cs.append(rcopy(s4.at[xh, part(c)], s4.at[xh, part(c)], c, 13 + k, p))
-        return cs
+        return [rcopy(s4.at[part(c), xh], s4.at[part(c), xh], c, 27 + k, p)
+                for k in range(1, far) for o, p in [peer4(k)]]
 
     def c4in(c):
-        cs = []
-        for k in range(1, far):
-            o, p = peer4(far - k)
-            cs.append(rcopy(s4.at[xh, part(c)], s4.at[o, part(c)], c, 13 + k, p))
-        return cs
+        return [rcopy(s4.at[part(c), xh], s4.at[part(c), o], c, 27 + k, p)
+                for k in range(1, far) for o, p in [peer4(far - k)]]
+
+    def c8(c):
+        return [rcopy(s8.at[part(c), oh, oq], r8.at[part(c), k], c, 13 + k, p)
+                for k in range(1, 8) for oh, oq, p in [peer8(k)]]
 
     def g3(c, inn=False):
-        cs = []
-        for k in (1, 2, 3):
-            o, p = peer3(4 - k if inn else k)
-            cs.append(rcopy(fin.at[h, q, y, part(c)], fin.at[h, q, o if inn else y, part(c)], c, 6 + k, p))
-        return cs
+        return [rcopy(fin.at[part(c), h, q, y], fin.at[part(c), h, q, o if inn else y], c, 6 + k, p)
+                for k in (1, 2, 3) for o, p in [peer3(4 - k if inn else k)]]
 
     def g2(c, inn=False):
-        cs = []
-        for k in (1, 2, 3):
-            o, p = peer2(4 - k if inn else k)
-            cs.append(rcopy(fin.at[h, q, :, part(c)], fin.at[h, o if inn else q, :, part(c)], c, 9 + k, p))
-        return cs
+        return [rcopy(fin.at[part(c), h, q], fin.at[part(c), h, o if inn else q], c, 9 + k, p)
+                for k in (1, 2, 3) for o, p in [peer2(4 - k if inn else k)]]
 
     def g1(c, inn=False):
-        return [rcopy(fin.at[h, :, :, part(c)], fin.at[1 - h if inn else h, :, :, part(c)], c, 13, peer1())]
+        return [rcopy(fin.at[part(c), h], fin.at[part(c), 1 - h if inn else h], c, 13, peer1())]
+
+    def g8(c, inn=False):
+        return [rcopy(fin.at[part(c), h, q], fin.at[part(c), oh if inn else h, oq if inn else q],
+                      c, 20 + k, p)
+                for k in range(1, 8) for oh, oq, p in [peer8(8 - k if inn else k)]]
 
     def start(cs):
         for r in cs:
@@ -266,39 +262,52 @@
             r.wait_recv()
 
     def st0(c):
-        s1[:, part(c)] = g_ref[1 - h, :, part(c)].astype(BF)
+        s1[part(c)] = g_ref[part(c), 1 - h].astype(BF)
         start(c1(c))
 
     def st1(c):
         landed(c1(c))
-        v = g_ref[h, :, part(c)] + r1[:, part(c)].astype(F32)
-        v = v.reshape((4, 4) + v.shape[1:])
-        a1[:, :, part(c)] = v
-        s2[:, :, part(c)] = v.astype(BF)
+        v = g_ref[part(c), h] + r1[part(c)].astype(F32)
+        a1[part(c)] = v
+        s2[part(c)] = v.astype(BF)
         start(c2(c))
+
+    def onward(c, v):
+        a2[part(c)] = v
+        s3[part(c)] = v.astype(BF)
+        start(c3(c))
 
     def st2(c):
         landed(c2(c))
-        v = a1[q, :, part(c)]
+        v = a1[part(c), q]
         for k in (1, 2, 3):
-            v = v + r2[k, :, part(c)].astype(F32)
-        a2[:, part(c)] = v
-        s3[:, part(c)] = v.astype(BF)
-        start(c3(c))
+            v = v + r2[part(c), k].astype(F32)
+        onward(c, v)
+
+    def w0(c):
+        s8[part(c)] = g_ref[part(c)].astype(BF)
+        start(c8(c))
+
+    def w1(c):
+        landed(c8(c))
+        v = g_ref[part(c), h, q]
+        for k in range(1, 8):
+            v = v + r8[part(c), k].astype(F32)
+        onward(c, v)
 
     def st3(c):
         landed(c3(c))
-        v = a2[y, part(c)]
+        v = a2[part(c), y]
         for k in (1, 2, 3):
-            v = v + r3[k, part(c)].astype(F32)
+            v = v + r3[part(c), k].astype(F32)
         if far > 1:
-            s4[xh, part(c)] = v.astype(BF)
+            s4[part(c), xh] = v.astype(BF)
             start(c4(c))
             landed(c4in(c))
-            v = s4[0, part(c)].astype(F32)
+            v = s4[part(c), 0].astype(F32)
             for k in range(1, far):
-                v = v + s4[k, part(c)].astype(F32)
-        fin[h, q, y, part(c)] = v.astype(BF)
+                v = v + s4[part(c), k].astype(F32)
+        fin[part(c), h, q, y] = v.astype(BF)
         start(g3(c))
 
     def st4(c):
@@ -309,40 +318,51 @@
         landed(g2(c, True))
         start(g1(c))
 
-    def st6(c):
-        landed(g1(c, True))
+    def result(c):
         off, size = chunks[c]
         for pos in range(4 * off, 4 * (off + size)):
             k = pos % 4
-            tile = fin[k // 2, 2 * (k % 2):2 * (k % 2) + 2, :, pos // 4].reshape(ch, ch)
-            if pos < 27:
-                gw_ref[(pos % 3) * 9 + pos // 3] = tile.astype(F32)
-            else:
-                gb_ref[...] = tile[0:16].astype(F32)[0:1]
-
-    st = [st0, st1, st2, st3, st4, st5, st6]
+            tile = fin[pos // 4, k // 2, 2 * (k % 2):2 * (k % 2) + 2].reshape(ch, ch)
+            gw_ref[(pos % 3) * 9 + pos // 3 if pos < 27 else 27] = tile.astype(F32)
+
+    def st6(c):
+        landed(g1(c, True))
+        result(c)
+
+    def w3(c):
+        landed(g3(c, True))
+        start(g8(c))
+
+    def w4(c):
+        landed(g8(c, True))
+        result(c)
+
+    far_way = [st0, st1, st2, st3, st4, st5, st6]
+    short_way = [w0, w1, st3, w3, w4]
+    way = [far_way, far_way, short_way, short_way]
     acc[...] = jnp.zeros(acc.shape, F32)
     n = (nx + 2) // 2
     put(27, jnp.broadcast_to(gb, (ch, ch)))
-    ready = {0: (0,), 1: (1, 2), 2: (3,), 3: (4, 5), 4: (6,)}
+    ready = {1: (0,), 2: (1,), 3: (2,), 4: (3,)}
     at = {}
     step = 0
-    while step < 5 or any(v < 7 for v in at.values()):
+    while step < 5 or any(v < len(way[c]) for c, v in at.items()):
         if step < 5:
             q0, q1 = 2 * step, min(2 * step + 2, 9)
             grad(q0, q1, 0, n)
             tiles(q0, q1)
         for c in sorted(at):
-            if at[c] < 7:
-                st[at[c]](c)
+            if at[c] < len(way[c]):
+                way[c][at[c]](c)
                 at[c] += 1
         for c in ready.get(step, ()):
-            st[0](c)
+            way[c][0](c)
             at[c] = 1
         step += 1
     store.wait()
     for c in range(len(chunks)):
-        for cs in (c1(c), c2(c), c3(c), c4(c), g3(c), g2(c), g1(c)):
+        long = way[c] is far_way
+        for cs in (c3(c), c4(c), g3(c)) + ((c1(c), c2(c), g2(c), g1(c)) if long else (c8(c), g8(c))):
             for r in cs:
                 r.wait_send()
 
@@ -351,33 +371,33 @@
     _, nx, ny, nz, ch = volume.shape
     blocks = block_active.shape[3]
     rows = ny * nz
-    chunks = tuple((k, 1) for k in range(7))
+    chunks = ((0, 3), (3, 1), (4, 2), (6, 1))
     far = max(nsx // 2, 1)
     anyw = pl.BlockSpec(memory_space=pl.ANY)
-    gr = (7, 16, ch)
+    gr = (16, ch)
     bf = lambda *dims: pltpu.VMEM(dims, BF)
     dma = pltpu.SemaphoreType.DMA
-    out, gw, gb = pl.pallas_call(
+    out, gw = pl.pallas_call(
         functools.partial(layer_kernel, nsx, nsy, nz // blocks, chunks),
         out_shape=(jax.ShapeDtypeStruct((nx, rows, ch), BF),
-                   jax.ShapeDtypeStruct((27, ch, ch), F32),
-                   jax.ShapeDtypeStruct((1, ch), F32)),
-        in_specs=[SM, VM, anyw, anyw, anyw], out_specs=(anyw, VM, VM),
+                   jax.ShapeDtypeStruct((28, ch, ch), F32)),
+        in_specs=[SM, VM, anyw, anyw, anyw], out_specs=(anyw, VM),
         scratch_shapes=[
             bf(2, ny, nz, ch), bf(2, nx, nz, ch), bf(2, ny, nz, ch), bf(2, nx + 2, nz, ch),
             bf(nx, ny, nz, ch), bf(36 * ch, 2 * ch), bf(nx, rows, ch), bf(nx, rows, ch),
             bf(nx + 2, rows + 2 * nz, 3 * ch), bf((nx + 4) * ch, rows), pltpu.VMEM((3 * ch, 9 * ch), F32),
             pltpu.VMEM((rows, 2 * ch), F32), pltpu.VMEM((rows, 2 * ch), F32),
-            pltpu.VMEM((2, 16) + gr, F32), bf(16, *gr), bf(16, *gr), pltpu.VMEM((4, 4) + gr, F32),
-            bf(4, 4, *gr), bf(4, 4, *gr), pltpu.VMEM((4,) + gr, F32), bf(4, *gr), bf(4, *gr),
-            bf(far, *gr), bf(2, 4, 4, *gr), dma((9,)), dma((8,)), dma((8,)),
-            dma((len(chunks), 13 + far)), dma((len(chunks), 13 + far))],
+            pltpu.VMEM((7, 2, 4, 4) + gr, F32), bf(7, 4, 4, *gr), bf(7, 4, 4, *gr),
+            pltpu.VMEM((7, 4, 4) + gr, F32), bf(7, 4, 4, *gr), bf(7, 4, 4, *gr),
+            pltpu.VMEM((7, 4) + gr, F32), bf(7, 4, *gr), bf(7, 4, *gr), bf(7, far, *gr),
+            bf(7, 2, 4, 4, *gr), bf(7, 8, 4, *gr), bf(7, 2, 4, 4, *gr), dma((9,)), dma((8,)), dma((8,)),
+            dma((len(chunks), 27 + far)), dma((len(chunks), 27 + far))],
         compiler_params=pltpu.CompilerParams(collective_id=0, has_side_effects=True,
                                              vmem_limit_bytes=60 * 2**20),
         name="layer",
     )(block_active.reshape(blocks), bias[None], volume[0],
       weight.reshape(27 * ch, ch), cotangent.reshape(nx, rows, ch))
-    return (out.reshape(volume.shape), gw.reshape(weight.shape), gb.reshape(ch))
+    return (out.reshape(volume.shape), gw[:27].reshape(weight.shape), gw[27, 0])
 
 
 def solution(mesh):

time: 70.1 us -> 68 us (0.970)
  Pallas kernels: 64 us -> 61.6 us
    unnamed x7 -> x3, local copies, waits for them, and re-layouts: 5.23 us -> 1.32 us
    slice x0 -> x1, local copies, waits for them, and re-layouts: none -> 3.02 us  [local(): return (out.reshape(volume.shape), gw[:27].reshape(weight.shape), gw[27, 0])]
    pallas_call x1, Pallas kernels: 64 us -> 61.6 us  [local(): pl.pallas_call(functools.partial(layer_kernel, nsx, nsy, nz // blocks, ch...]
    squeeze x0 -> x1, local copies, waits for them, and re-layouts: none -> 1.19 us  [local(): return (out.reshape(volume.shape), gw[:27].reshape(weight.shape), gw[27, 0])]
where the time goes in v4:
time: 68 us; the launch traced here: 67.8 us
  Pallas kernels  61.6 us (91%)
  local copies, waits for them, and re-layouts  5.54 us (8%)
    pallas_call x1, Pallas kernels, local(): pl.pallas_call(functools.partial(layer_kernel, nsx, nsy, nz // blocks, ch...  61.6 us
    slice x1, local copies, waits for them, and re-layouts, local(): return (out.reshape(volume.shape), gw[:27].reshape(weight.shape), gw[27, 0])  3.02 us

profile of v4, /device:TPU:0, one launch (start us, length us, event | category | flops | bytes accessed | tf_op | source)
XLA Modules:
  0.0 67.8 jit_solution(4520844104866210171)
XLA Ops:
  0.6 61.6 %layer.1 = (bf16[16,512,128]{2,1,0:T(8,128)(2,1)}, f32[28,128,128]{2,1,0:T(8,128)}) custom-call(s32[2]{0:T(128)} %bitcast.14, f32[1,128]{1,0:T(1,128)} %bitcast.15, bf16[16,16,32,128]{3,2,1,0:T(8,128)(2,1)} %bitcast.9, bf16[3456,128]{1,0:T(8,128)(2,1)} %bitcast.13, bf16[16,512,128]{2,1,0:T(8,128)(2,1)} %bitcast.10), custom_call_target="tpu_custom_call" | custom-call | tf_op jit(solution)/shard_map/layer/pallas_call | solution.py:380
  62.2 0.0 copy-start
  62.2 3.0 %slice.6 = f32[27,128,128]{2,1,0:T(8,128)} slice(f32[28,128,128]{2,1,0:T(8,128)} %get-tuple-element.6), slice={[0:27], [0:128], [0:128]} | slice | bytes 3538944 | tf_op jit(solution)/shard_map/slice | solution.py:400
  65.2 1.2 %slice_bitcast_fusion = f32[128]{0:T(128)} fusion(f32[28,128,128]{2,1,0:T(8,128)} %get-tuple-element.6), kind=kLoop, calls=%fused_computation | loop fusion | bytes 1024 | tf_op jit(solution)/shard_map/squeeze | solution.py:400
  66.4 0.0 copy-done
  66.4 1.3 %copy.9 = bf16[1,16,16,32,128]{4,3,2,1,0:T(8,128)(2,1)} copy(bf16[1,16,16,32,128]{4,3,2,1,0:T(8,128)(2,1)S(1)} %bitcast.11) | data formatting | bytes 4194304
Async XLA Ops:
  62.2 4.2 %copy-start = (bf16[16,512,128]{2,1,0:T(8,128)(2,1)S(1)}, bf16[16,512,128]{2,1,0:T(8,128)(2,1)}, u32[]{:S(2)}) copy-start(bf16[16,512,128]{2,1,0:T(8,128)(2,1)} %get-tuple-element.5) | copy-start | bytes 6291460

commit v5 on v4

--- a/solution.py
+++ b/solution.py
@@ -373,7 +373,7 @@
     rows = ny * nz
     chunks = ((0, 3), (3, 1), (4, 2), (6, 1))
     far = max(nsx // 2, 1)
-    anyw = pl.BlockSpec(memory_space=pl.ANY)
+    anyw = pl.BlockSpec(memory_space=pltpu.HBM)
     gr = (16, ch)
     bf = lambda *dims: pltpu.VMEM(dims, BF)
     dma = pltpu.SemaphoreType.DMA
@@ -393,7 +393,7 @@
             bf(7, 2, 4, 4, *gr), bf(7, 8, 4, *gr), bf(7, 2, 4, 4, *gr), dma((9,)), dma((8,)), dma((8,)),
             dma((len(chunks), 27 + far)), dma((len(chunks), 27 + far))],
         compiler_params=pltpu.CompilerParams(collective_id=0, has_side_effects=True,
-                                             vmem_limit_bytes=60 * 2**20),
+                                             vmem_limit_bytes=40 * 2**20),
         name="layer",
     )(block_active.reshape(blocks), bias[None], volume[0],
       weight.reshape(27 * ch, ch), cotangent.reshape(nx, rows, ch))

time: 68 us -> 70.1 us (1.031)
  local copies, waits for them, and re-layouts: 5.54 us -> 8.81 us
  Pallas kernels: 61.6 us -> 60.4 us
    unnamed x3 -> x11, local copies, waits for them, and re-layouts: 1.32 us -> 6.97 us
    slice x1, local copies, waits for them, and re-layouts: 3.02 us -> 1.33 us  [local(): return (out.reshape(volume.shape), gw[:27].reshape(weight.shape), gw[27, 0])]
    pallas_call x1, Pallas kernels: 61.6 us -> 60.4 us  [local(): pl.pallas_call(functools.partial(layer_kernel, nsx, nsy, nz // blocks, ch...]
where the time goes in v5:
time: 70.1 us; the launch traced here: 69.8 us
  Pallas kernels  60.4 us (86%)
  local copies, waits for them, and re-layouts  8.81 us (13%)
    pallas_call x1, Pallas kernels, local(): pl.pallas_call(functools.partial(layer_kernel, nsx, nsy, nz // blocks, ch...  60.4 us
    unnamed x11, local copies, waits for them, and re-layouts  6.97 us

profile of v5, /device:TPU:0, one launch (start us, length us, event | category | flops | bytes accessed | tf_op | source)
XLA Modules:
  0.0 69.8 jit_solution(10526486795026640290)
XLA Ops:
  0.6 0.0 copy-start
  0.6 1.6 %copy-done = bf16[1,16,16,32,128]{4,3,2,1,0:T(8,128)(2,1)S(1)} copy-done((bf16[1,16,16,32,128]{4,3,2,1,0:T(8,128)(2,1)S(1)}, bf16[1,16,16,32,128]{4,3,2,1,0:T(8,128)(2,1)}, u32[]{:S(2)}) %copy-start) | copy-done | bytes 2097176
  2.2 0.0 copy-start.1
  2.2 1.6 %copy-done.1 = bf16[1,16,16,32,128]{4,3,2,1,0:T(8,128)(2,1)S(1)} copy-done((bf16[1,16,16,32,128]{4,3,2,1,0:T(8,128)(2,1)S(1)}, bf16[1,16,16,32,128]{4,3,2,1,0:T(8,128)(2,1)}, u32[]{:S(2)}) %copy-start.1) | copy-done | bytes 2097176
  3.8 0.0 copy-start.2
  3.8 1.2 %copy-done.2 = bf16[3,3,3,128,128]{4,3,2,1,0:T(8,128)(2,1)S(1)} copy-done((bf16[3,3,3,128,128]{4,3,2,1,0:T(8,128)(2,1)S(1)}, bf16[3,3,3,128,128]{4,3,2,1,0:T(8,128)(2,1)}, u32[]{:S(2)}) %copy-start.2) | copy-done | bytes 884760
  5.0 0.0 copy-start.3
  5.0 0.7 copy-done.3
  5.6 0.0 copy-start.4
  5.6 0.7 copy-done.4
  6.3 60.4 %layer.1 = (bf16[16,512,128]{2,1,0:T(8,128)(2,1)S(1)}, f32[28,128,128]{2,1,0:T(8,128)S(1)}) custom-call(s32[2]{0:T(128)S(1)} %bitcast.13, f32[1,128]{1,0:T(1,128)S(1)} %bitcast.14, bf16[16,16,32,128]{3,2,1,0:T(8,128)(2,1)S(1)} %bitcast.9, bf16[3456,128]{1,0:T(8,128)(2,1)S(1)} %bitcast.12, bf16[16,512,128]{2,1,0:T(8,128)(2,1)S(1)} %bitcast.10), custom_call_target="tpu_custom_call" | custom-call | tf_op jit(solution)/shard_map/layer/pallas_call | solution.py:380
  66.7 1.3 %slice.6 = f32[27,128,128]{2,1,0:T(8,128)} slice(f32[28,128,128]{2,1,0:T(8,128)S(1)} %get-tuple-element.6), slice={[0:27], [0:128], [0:128]} | slice | bytes 3538944 | tf_op jit(solution)/shard_map/slice | solution.py:400
  68.0 0.5 slice_bitcast_fusion
  68.5 1.3 %copy.9 = bf16[1,16,16,32,128]{4,3,2,1,0:T(8,128)(2,1)} copy(bf16[1,16,16,32,128]{4,3,2,1,0:T(8,128)(2,1)S(1)} %bitcast.11) | data formatting | bytes 4194304
Async XLA Ops:
  0.6 1.6 %copy-start = (bf16[1,16,16,32,128]{4,3,2,1,0:T(8,128)(2,1)S(1)}, bf16[1,16,16,32,128]{4,3,2,1,0:T(8,128)(2,1)}, u32[]{:S(2)}) copy-start(bf16[1,16,16,32,128]{4,3,2,1,0:T(8,128)(2,1)} %param.5) | copy-start | bytes 6291460
  2.2 1.6 %copy-start.1 = (bf16[1,16,16,32,128]{4,3,2,1,0:T(8,128)(2,1)S(1)}, bf16[1,16,16,32,128]{4,3,2,1,0:T(8,128)(2,1)}, u32[]{:S(2)}) copy-start(bf16[1,16,16,32,128]{4,3,2,1,0:T(8,128)(2,1)} %param.9) | copy-start | bytes 6291460
  3.8 1.2 %copy-start.2 = (bf16[3,3,3,128,128]{4,3,2,1,0:T(8,128)(2,1)S(1)}, bf16[3,3,3,128,128]{4,3,2,1,0:T(8,128)(2,1)}, u32[]{:S(2)}) copy-start(bf16[3,3,3,128,128]{4,3,2,1,0:T(8,128)(2,1)} %param.7) | copy-start | bytes 2654212
  5.0 0.7 copy-start.3
  5.6 0.7 copy-start.4
